TPU v7x, 32 devices: a whole 2x2x4 slice. The times are simulated.
32 devices in a mesh: groups: 2 (over y), rows: 4 (over z), angle: 4 (over x, core).
Axes of the slice: x: 2, y: 2, z: 4, core: 2. Of those that a mesh axis runs over, the one named last changes fastest.
Arguments:
- projections: float32 [16, 512, 4096], P(('groups', 'angle'), 'rows'), parts along dimension 0, may hold values from 0 to 6
- rowmap: int32 [16, 256], P(('groups', 'angle')), parts along dimension 0, may hold values from 0 to 511, as said below
- offsets: int32 [16, 8192], P(('groups', 'angle')), parts along dimension 0, may hold values from 0 to 4094
- fractions: float32 [16, 8192], P(('groups', 'angle')), parts along dimension 0, may hold values from 0 to 1
- distance_weight: float32 [16, 8192], P(('groups', 'angle')), parts along dimension 0, may hold values from 0.5 to 2
Outputs:
- volume: float32 [512, 8192], P(('groups', 'rows'), 'angle'), parts along dimension 0
There are 2 independent parts, one for each index of `groups`. A program takes and returns all parts, laid end to end along the dimension named above; each array names one. Nothing has to cross between parts.
Inputs may be any that keep to these rules, and one draw needn't show every extreme that they name: `rowmap`: the plane stored at index k * 64 + m is the physical plane q = m * 4 + k, and in every projection it reads a row from 2 * q to 2 * q + 1.
All inputs are finite; a program needn't handle non-finite values.
Results may differ from a plain program's by a relative error of at most 0.0004.
The roundings to bfloat16 on the way count: a program that leaves them out, or rounds other values in their place, can miss the bound.
Values may be sent and summed in bfloat16 or wider, within the bound.
A program may use at most 128 MiB of HBM per device.

v0:
```python
import math

import jax
import jax.numpy as jnp
from jax import lax
from jax.sharding import PartitionSpec as P


def ramp_table(offset):
    magnitude = jnp.abs(offset)
    spread = jnp.maximum(magnitude, 1).astype(jnp.float32)
    odd_term = -1.0 / (math.pi**2 * spread * spread)
    value = jnp.where(magnitude == 0, 0.25, jnp.where(magnitude % 2 == 1, odd_term, 0.0))
    return value.astype(jnp.bfloat16)


def ramp_filter(rows):
    width = rows.shape[-1]
    flat = rows.reshape(-1, width)
    block = min(512, width)
    pieces = []
    for first in range(0, width, block):
        source = lax.broadcasted_iota(jnp.int32, (width, block), 0)
        target = lax.broadcasted_iota(jnp.int32, (width, block), 1) + first
        table = ramp_table(target - source)
        pieces.append(jnp.dot(flat, table, preferred_element_type=jnp.float32))
    return jnp.concatenate(pieces, axis=1).astype(jnp.bfloat16).reshape(rows.shape)


def cone_weight(row_value, width, height):
    column = jnp.arange(width, dtype=jnp.float32) - (width - 1) / 2.0
    vertical = row_value - (height - 1) / 2.0
    distance = 2.0 * width
    return distance / jnp.sqrt(distance * distance + column * column + vertical * vertical)


def take_rows(stack, index):
    return jax.vmap(lambda plane_set, chosen: jnp.take(plane_set, chosen, axis=0))(stack, index)


def view_terms(selected, offset, fraction, weight):
    planes = selected.shape[0]
    flipped = selected.T
    following = jnp.concatenate([flipped[1:], flipped[-1:]], axis=0)
    paired = jnp.concatenate([flipped, following], axis=1)
    both = jnp.take(paired, offset, axis=0).astype(jnp.float32)
    lower = both[:, :planes]
    upper = both[:, planes:]
    return (weight * (1.0 - fraction))[:, None] * lower + (weight * fraction)[:, None] * upper


def backproject(selected, offsets, fractions, distance_weight):
    terms = jax.vmap(view_terms)(selected, offsets, fractions, distance_weight)
    return jnp.sum(terms, axis=0).T


def local(projections, rowmap, offsets, fractions, distance_weight):
    bands = lax.axis_size("rows")
    here = lax.axis_index("rows")
    proj_count, band, width = projections.shape
    zdev = rowmap.shape[1] // bands
    capacity = zdev // bands
    height = band * bands
    global_rows = (here * band + jnp.arange(band, dtype=jnp.int32)).astype(jnp.float32)
    weighted = (projections * cone_weight(global_rows[None, :, None], width, height)).astype(
        jnp.bfloat16
    )
    outgoing = ramp_filter(weighted)
    grouped = rowmap.reshape(proj_count, bands, zdev)
    wanted = lax.dynamic_slice_in_dim(grouped, here * capacity, capacity, 2)
    slot_local = jnp.clip(wanted - here * band, 0, band - 1).reshape(proj_count, bands * capacity)
    picked = take_rows(outgoing, slot_local)
    arrived = lax.all_to_all(picked, "rows", split_axis=1, concat_axis=1, tiled=True)
    partial_sum = backproject(arrived, offsets, fractions, distance_weight)
    return lax.psum_scatter(partial_sum, "angle", scatter_dimension=1, tiled=True)


def solution(mesh):
    in_specs = (
        P(("groups", "angle"), "rows", None),
        P(("groups", "angle"), None),
        P(("groups", "angle"), None),
        P(("groups", "angle"), None),
        P(("groups", "angle"), None),
    )
    out_specs = P(("groups", "rows"), "angle")
    return jax.shard_map(local, mesh=mesh, in_specs=in_specs, out_specs=out_specs, check_vma=False)
```

profile of v0, /device:TPU:0, one launch (start us, length us, event | category | flops | bytes accessed | tf_op | source)
XLA Modules:
  0.0 355.0 jit_solution(10893682259361557686)
XLA Ops:
  6.6 0.6 iota_add_fusion
  7.2 0.8 reshape.126
  8.0 0.1 subtract_clamp_fusion
  8.1 0.1 reshape.128
  8.1 0.1 reshape.127
  8.2 0.5 rsqrt_multiply_fusion
  8.7 2.6 multiply_convert_fusion
  11.3 0.0 copy-start.2
  11.4 7.8 %fusion.119 = bf16[2,128,4096]{2,1,0:T(8,128)(2,1)S(1)} fusion(bf16[2,128,4096]{2,1,0:T(8,128)(2,1)S(1)} %multiply_convert_fusion), kind=kOutput, calls=%fused_computation.144 | convolution fusion | flops 1122107392 | bytes 2359296 | tf_op jit(solution)/shard_map/dot_general | solution.py:26
  19.2 0.0 copy-done.2
  19.2 0.7 reshape.129
  19.9 0.7 copy.7
  20.6 9.6 %fusion.140 = bf16[2,128,4096]{2,1,0:T(8,128)(2,1)S(1)} fusion(bf16[2,128,4096]{2,1,0:T(8,128)(2,1)S(1)} %fusion.119, bf16[2,128,4096]{2,1,0:T(8,128)(2,1)} %copy-done.2, s32[512]{0:T(512)S(1)} %iota_add_fusion.6), kind=kOutput, calls=%fused_computation.151 | convolution fusion | flops 1122107392 | bytes 2361344 | tf_op jit(solution)/shard_map/dot_general | solution.py:26
  30.2 0.0 copy-done.3
  30.2 8.4 %fusion.137 = bf16[2,128,4096]{2,1,0:T(8,128)(2,1)S(1)} fusion(bf16[2,128,4096]{2,1,0:T(8,128)(2,1)S(1)} %fusion.140, bf16[2,128,4096]{2,1,0:T(8,128)(2,1)S(1)} %copy-done.3, s32[512]{0:T(512)S(1)} %iota_add_fusion.5), kind=kOutput, calls=%fused_computation.150 | convolution fusion | flops 1122107392 | bytes 2361344 | tf_op jit(solution)/shard_map/dot_general | solution.py:26
  38.6 7.9 %fusion.134 = bf16[2,128,4096]{2,1,0:T(8,128)(2,1)S(1)} fusion(bf16[2,128,4096]{2,1,0:T(8,128)(2,1)S(1)} %fusion.137, bf16[2,128,4096]{2,1,0:T(8,128)(2,1)S(1)} %copy-done.3, s32[512]{0:T(512)S(1)} %iota_add_fusion.4), kind=kOutput, calls=%fused_computation.149 | convolution fusion | flops 1122107392 | bytes 2361344 | tf_op jit(solution)/shard_map/dot_general | solution.py:26
  46.4 8.0 %fusion.131 = bf16[2,128,4096]{2,1,0:T(8,128)(2,1)S(1)} fusion(bf16[2,128,4096]{2,1,0:T(8,128)(2,1)S(1)} %fusion.134, bf16[2,128,4096]{2,1,0:T(8,128)(2,1)S(1)} %copy-done.3, s32[512]{0:T(512)S(1)} %iota_add_fusion.3), kind=kOutput, calls=%fused_computation.148 | convolution fusion | flops 1122107392 | bytes 2361344 | tf_op jit(solution)/shard_map/dot_general | solution.py:26
  54.5 7.9 %fusion.128 = bf16[2,128,4096]{2,1,0:T(8,128)(2,1)S(1)} fusion(bf16[2,128,4096]{2,1,0:T(8,128)(2,1)S(1)} %fusion.131, bf16[2,128,4096]{2,1,0:T(8,128)(2,1)S(1)} %copy-done.3, s32[512]{0:T(512)S(1)} %iota_add_fusion.2), kind=kOutput, calls=%fused_computation.147 | convolution fusion | flops 1122107392 | bytes 2361344 | tf_op jit(solution)/shard_map/dot_general | solution.py:26
  62.3 0.0 copy-start.8
  62.3 8.1 %fusion.125 = bf16[2,128,4096]{2,1,0:T(8,128)(2,1)S(1)} fusion(bf16[2,128,4096]{2,1,0:T(8,128)(2,1)S(1)} %fusion.128, bf16[2,128,4096]{2,1,0:T(8,128)(2,1)S(1)} %copy-done.3, s32[512]{0:T(512)S(1)} %iota_add_fusion.1), kind=kOutput, calls=%fused_computation.146 | convolution fusion | flops 1122107392 | bytes 2361344 | tf_op jit(solution)/shard_map/dot_general | solution.py:26
  70.4 0.0 copy-done.8
  70.4 0.0 copy-start.1
  70.4 8.1 %fusion.122 = bf16[2,128,4096]{2,1,0:T(8,128)(2,1)S(1)} fusion(bf16[2,128,4096]{2,1,0:T(8,128)(2,1)S(1)} %fusion.125, bf16[2,128,4096]{2,1,0:T(8,128)(2,1)S(1)} %copy-done.3, s32[512]{0:T(512)S(1)} %copy-done.8), kind=kOutput, calls=%fused_computation.145 | convolution fusion | flops 1122107392 | bytes 2361344 | tf_op jit(solution)/shard_map/dot_general | solution.py:26
  78.6 0.0 copy-done.1
  78.6 0.0 copy-start.7
  78.6 0.0 copy-start.4
  78.6 0.0 copy-start.5
  78.6 0.0 copy-start.6
  78.6 3.9 %gather_fusion = bf16[128,4096]{1,0:T(8,128)(2,1)S(1)} fusion(bf16[2,128,4096]{2,1,0:T(8,128)(2,1)S(1)} %fusion.122, s32[128]{0:T(128)S(1)} %copy-done.1), kind=kCustom, calls=%fused_computation | custom fusion | bytes 2098176 | tf_op jit(solution)/shard_map/vmap(jit(_take))/gather | solution.py:38
  82.5 0.0 copy-done.7
  82.5 2.3 broadcast_select_fusion
  84.8 6.3 %all-to-all-start = ((bf16[2,64,4096]{2,0,1:T(2,128)(2,1)}), bf16[2,64,4096]{2,0,1:T(2,128)(2,1)S(1)}, u32[]{:S(2)}, u32[]{:S(2)}) async-start(bf16[2,64,4096]{2,0,1:T(2,128)(2,1)} %broadcast_select_fusion), calls=%async_computation | async-start | bytes 2097152 | tf_op jit(solution)/shard_map/all_to_all | solution.py:73
  91.1 0.0 reduce-scatter.2.cloned.1.call-start
  91.1 0.0 copy-done.4
  91.1 0.1 fusion.143
  91.3 0.1 subtract_multiply_fusion
  91.3 0.1 compare_and_fusion
  91.4 25.4 %all-to-all-done = bf16[2,64,4096]{2,0,1:T(2,128)(2,1)S(1)} async-done(((bf16[2,64,4096]{2,0,1:T(2,128)(2,1)}), bf16[2,64,4096]{2,0,1:T(2,128)(2,1)S(1)}, u32[]{:S(2)}, u32[]{:S(2)}) %all-to-all-start) | async-done | bytes 1048608 | tf_op jit(solution)/shard_map/all_to_all | solution.py:73
  116.9 1.5 copy.9
  118.4 0.5 slice.20
  118.9 0.8 copy-done
  119.7 2.7 fusion.94
  122.4 159.0 %gather_fusion.1 = bf16[16384,128]{1,0:T(8,128)(2,1)} fusion(bf16[2,4096,128]{2,1,0:T(8,128)(2,1)S(1)} %fusion.94, s32[16384]{0:T(1024)S(1)} %bitcast.78), kind=kCustom, calls=%fused_computation.1 | custom fusion | bytes 8519680 | tf_op jit(solution)/shard_map/vmap(jit(_take))/gather | solution.py:46
  281.5 6.1 %select_convert_fusion = f32[2,8192,128]{2,1,0:T(8,128)S(1)} fusion(bf16[2,8192,128]{2,1,0:T(8,128)(2,1)} %bitcast.83, pred[2,8192]{1,0:T(4,128)(4,1)S(1)} %compare_and_fusion), kind=kLoop, calls=%fused_computation.113 | loop fusion | flops 4194304 | bytes 12599296 | tf_op jit(solution)/shard_map/vmap()/convert_element_type | solution.py:46
  287.5 14.2 %fusion.41 = f32[8192,64]{1,0:T(8,128)} fusion(f32[2,8192,128]{2,1,0:T(8,128)S(1)} %select_convert_fusion, f32[2,8192]{1,0:T(2,128)S(1)} %get-tuple-element.6, f32[2,8192]{1,0:T(2,128)S(1)} %get-tuple-element.5), kind=kLoop, calls=%fused_computation.76 | loop fusion | flops 3670016 | bytes 10616832 | tf_op jit(solution)/shard_map/reduce_sum | solution.py:54
  301.8 0.0 reduce-scatter.2.cloned.1.call-update
  301.8 43.8 %reduce-scatter.2.cloned.1.call-done = f32[64,2048]{0,1:T(8,128)} async-done(((f32[64,8192]{0,1:T(8,128)}), f32[64,2048]{0,1:T(8,128)}) %reduce-scatter.2.cloned.1.call-update) | async-done | bytes 524304 | tf_op jit(solution)/shard_map/reduce_scatter | solution.py:75
  345.5 2.3 copy.10
  (16 shorter events, 0.1 us)
Async XLA Ops:
  11.3 7.9 %copy-start.2 = (bf16[2,128,4096]{2,1,0:T(8,128)(2,1)}, bf16[2,128,4096]{2,1,0:T(8,128)(2,1)S(1)}, u32[]{:S(2)}) copy-start(bf16[2,128,4096]{2,1,0:T(8,128)(2,1)S(1)} %multiply_convert_fusion) | copy-start | bytes 6291460
  20.6 9.6 %copy-start.3 = (bf16[2,128,4096]{2,1,0:T(8,128)(2,1)S(1)}, bf16[2,128,4096]{2,1,0:T(8,128)(2,1)}, u32[]{:S(2)}) copy-start(bf16[2,128,4096]{2,1,0:T(8,128)(2,1)} %copy-done.2) | copy-start | bytes 6291460
  62.3 8.1 %copy-start.8 = (s32[512]{0:T(512)S(1)}, s32[512]{0:T(512)}, u32[]{:S(2)}) copy-start(s32[512]{0:T(512)} %iota_add_fusion) | copy-start | bytes 6148
  70.4 8.1 %copy-start.1 = (s32[128]{0:T(128)S(1)}, s32[128]{0:T(128)}, u32[]{:S(2)}) copy-start(s32[128]{0:T(128)} %reshape.129) | copy-start | bytes 1540
  78.6 3.9 %copy-start.7 = (pred[2,64]{0,1:T(8,128)(4,1)S(1)}, pred[2,64]{0,1:T(8,128)(4,1)}, u32[]{:S(2)}) copy-start(pred[2,64]{0,1:T(8,128)(4,1)} %copy.7) | copy-start | bytes 388
  78.6 12.6 %copy-start.4 = (s32[2,8192]{1,0:T(2,128)S(1)}, s32[2,8192]{1,0:T(2,128)}, u32[]{:S(2)}) copy-start(s32[2,8192]{1,0:T(2,128)} %param.7) | copy-start | bytes 196612
  78.6 12.7 %copy-start.5 = (f32[2,8192]{1,0:T(2,128)S(1)}, f32[2,8192]{1,0:T(2,128)}, u32[]{:S(2)}) copy-start(f32[2,8192]{1,0:T(2,128)} %param.9) | copy-start | bytes 196612
  78.6 12.7 %copy-start.6 = (f32[2,8192]{1,0:T(2,128)S(1)}, f32[2,8192]{1,0:T(2,128)}, u32[]{:S(2)}) copy-start(f32[2,8192]{1,0:T(2,128)} %param.8) | copy-start | bytes 196612
  84.8 32.0 %all-to-all-start = ((bf16[2,64,4096]{2,0,1:T(2,128)(2,1)}), bf16[2,64,4096]{2,0,1:T(2,128)(2,1)S(1)}, u32[]{:S(2)}, u32[]{:S(2)}) async-start(bf16[2,64,4096]{2,0,1:T(2,128)(2,1)} %broadcast_select_fusion), calls=%async_computation | async-start | bytes 2097152 | tf_op jit(solution)/shard_map/all_to_all | solution.py:73
  91.1 254.4 %reduce-scatter.2.cloned.1.call-start = ((), (), s32[]{:S(2)}) async-start(), calls=%async_computation.2 | async-start | bytes 5242880 | tf_op jit(solution)/shard_map/reduce_scatter | solution.py:75
  118.3 1.3 copy-start
Sparse Core Ops, SparseCore 0:
  301.9 43.5 reduce-scatter.1
where the time goes:
time: 362 us; the launch traced here: 355 us
  local copies, waits for them, and re-layouts  170 us (47%)
  waiting for transfers between devices  69.2 us (19%)
  matrix products  65.7 us (18%)
  other arithmetic  29.4 us (8%)
  between operations  14 us (4%)
  starting transfers between devices  6.32 us (2%)
    gather x1, local copies, waits for them, and re-layouts, view_terms(): both = jnp.take(paired, offset, axis=0).astype(jnp.float32)  159 us
    dot_general x8, matrix products, ramp_filter(): pieces.append(jnp.dot(flat, table, preferred_element_type=jnp.float32))  65.7 us
    reduce_scatter x1, waiting for transfers between devices, local(): lax.psum_scatter(partial_sum, 'angle', scatter_dimension=1, tiled=True)  43.8 us
    all_to_all x1, waiting for transfers between devices, local(): lax.all_to_all(picked, 'rows', split_axis=1, concat_axis=1, tiled=True)  25.4 us
    reduce_sum x1, other arithmetic, backproject(): return jnp.sum(terms, axis=0).T  14.2 us
  transfers between devices with their start and end apart: 2, of which 2 were waited for; matrix products, arithmetic and copies ran while one was open for 0% of the time, Pallas kernels for 0%

commit v1 on v0

v1 whole, which is shorter than its diff:
```python
import functools
import math

import jax
import jax.numpy as jnp
import ml_dtypes
import numpy as np
from jax import lax
from jax.experimental import pallas as pl
from jax.experimental.pallas import tpu as pltpu
from jax.sharding import PartitionSpec as P

BLOCK = 256
PIX = 128
GROUP = 32
MESH = pl.DeviceIdType.MESH


def ramp_values(lag):
    magnitude = np.abs(lag)
    spread = np.maximum(magnitude, 1).astype(np.float32)
    odd_term = np.float32(-1.0) / (np.float32(math.pi**2) * spread * spread)
    value = np.where(magnitude % 2 == 1, odd_term, np.float32(0.0))
    return value.astype(ml_dtypes.bfloat16)


def odd_lag_tables(width):
    half = width // 2
    blocks = half // BLOCK
    row = np.arange(BLOCK)[:, None]
    column = np.arange((2 * blocks - 1) * BLOCK)[None, :] - (blocks - 1) * BLOCK
    difference = row - column
    return np.stack([ramp_values(2 * difference - 1), ramp_values(2 * difference + 1)])


def kernel(
    dims,
    x_ref,
    chosen_ref,
    ramp_ref,
    idx_mine,
    idx_theirs,
    wgt_mine,
    wgt_theirs,
    out_ref,
    xt,
    te,
    to,
    tables,
    idx_smem,
    idx_recv,
    wgt_recv,
    rows_buf,
    stage,
    arrived,
    zstage,
    x_send,
    x_recv,
    idx_sems,
    part_send,
    part_recv,
    z_send,
    z_recv,
    smem_sems,
):
    angles, bands, band, width, zdev, npq, chunk = dims
    pairs = angles // 2
    capacity = zdev // bands
    chunks = npq // chunk
    half = width // 2
    height = band * bands
    rows2 = 2 * zdev
    me = lax.axis_index("angle")
    here = lax.axis_index("rows")
    my_pair = me // 2
    parity = me - 2 * my_pair
    partner = {"angle": 2 * my_pair + 1 - parity}

    def pair_peer(step):
        return lax.rem(my_pair + step, pairs)

    def band_peer(step):
        return lax.rem(here + step, bands)

    own_idx = pltpu.make_async_copy(
        idx_mine, idx_smem.at[pl.ds(0, 2 * pairs * npq)], smem_sems.at[0]
    )
    own_idx.start()

    barrier = pltpu.get_barrier_semaphore()
    pl.semaphore_signal(barrier, inc=1, device_id=partner, device_id_type=MESH)
    for step in range(1, pairs):
        pl.semaphore_signal(
            barrier,
            inc=1,
            device_id={"angle": 2 * pair_peer(step) + parity},
            device_id_type=MESH,
        )
    for step in range(1, bands):
        pl.semaphore_signal(
            barrier, inc=1, device_id={"rows": band_peer(step)}, device_id_type=MESH
        )
    pl.semaphore_wait(barrier, pairs + bands - 1)

    send_idx = pltpu.make_async_remote_copy(
        idx_theirs, idx_recv, idx_sems.at[0], idx_sems.at[1], device_id=partner, device_id_type=MESH
    )
    send_idx.start()
    send_wgt = pltpu.make_async_remote_copy(
        wgt_theirs, wgt_recv, idx_sems.at[2], idx_sems.at[3], device_id=partner, device_id_type=MESH
    )
    send_wgt.start()

    lane_row = lax.broadcasted_iota(jnp.int32, (zdev, band), 1)
    select = [
        (chosen_ref[p * zdev : (p + 1) * zdev, :] == lane_row).astype(jnp.bfloat16)
        for p in range(2)
    ]
    target = lax.broadcasted_iota(jnp.int32, (BLOCK, BLOCK), 0)
    source = lax.broadcasted_iota(jnp.int32, (BLOCK, BLOCK), 1)
    wanted = jnp.where(target < BLOCK // 2, 2 * target, 2 * target - BLOCK + 1)
    unshuffle = (wanted == source).astype(jnp.bfloat16)
    row_value = (here * band + lax.broadcasted_iota(jnp.int32, (band, 1), 0)).astype(jnp.float32)
    vertical = row_value - (height - 1) / 2.0
    vertical_square = vertical * vertical
    distance = 2.0 * width

    for block in range(width // BLOCK):
        first = block * BLOCK
        column = lax.broadcasted_iota(jnp.int32, (1, BLOCK), 1).astype(jnp.float32) + (
            first - (width - 1) / 2.0
        )
        cosine = distance / jnp.sqrt(distance * distance + column * column + vertical_square)
        picked = []
        for p in range(2):
            weighted = (x_ref[p, :, first : first + BLOCK] * cosine).astype(jnp.bfloat16)
            picked.append(jnp.dot(select[p], weighted, preferred_element_type=jnp.float32))
        picked = jnp.concatenate(picked, axis=0).astype(jnp.bfloat16)
        turned = lax.dot_general(
            unshuffle, picked, (((1,), (1,)), ((), ())), preferred_element_type=jnp.float32
        ).astype(jnp.bfloat16)
        at = block * (BLOCK // 2)
        xt[0, at : at + BLOCK // 2, 0:rows2] = turned[: BLOCK // 2]
        xt[1, at : at + BLOCK // 2, 0:rows2] = turned[BLOCK // 2 :]

    send_x = pltpu.make_async_remote_copy(
        xt.at[:, :, pl.ds(0, rows2)],
        xt.at[:, :, pl.ds(rows2, rows2)],
        x_send,
        x_recv,
        device_id=partner,
        device_id_type=MESH,
    )
    send_x.start()

    send_idx.wait_recv()
    other_idx = pltpu.make_async_copy(
        idx_recv, idx_smem.at[pl.ds(2 * pairs * npq, 2 * pairs * npq)], smem_sems.at[1]
    )
    other_idx.start()

    send_x.wait()

    blocks = half // BLOCK
    for block in range(blocks):
        start = (blocks - 1 - block) * BLOCK
        at = block * BLOCK
        for side, out in ((0, te), (1, to)):
            total = jnp.dot(
                ramp_ref[side, :, start : start + half],
                xt[1 - side],
                preferred_element_type=jnp.float32,
            )
            total = total + 0.25 * xt[side, at : at + BLOCK, :].astype(jnp.float32)
            out[at : at + BLOCK, :] = total.astype(jnp.bfloat16).astype(jnp.float32)
    te[half : half + 8, :] = jnp.zeros((8, 2 * rows2), jnp.float32)

    low = lax.broadcasted_iota(jnp.int32, (BLOCK, rows2), 1) < zdev

    def build(block, carry):
        at = pl.multiple_of(block * BLOCK, BLOCK)
        for side in range(2):
            lanes = slice(side * rows2, (side + 1) * rows2)
            even = te[pl.ds(at, BLOCK), lanes]
            odd = to[pl.ds(at, BLOCK), lanes]
            later = te[pl.ds(at, BLOCK + 8), lanes][1 : BLOCK + 1]
            turned_odd = pltpu.roll(odd, zdev, 1)
            tables[2 * side, pl.ds(at, BLOCK), :] = jnp.where(low, even, turned_odd)
            tables[2 * side + 1, pl.ds(at, BLOCK), :] = jnp.where(
                low, pltpu.roll(even, zdev, 1), odd
            )
            tables[2 * side, pl.ds(half + at, BLOCK), :] = jnp.where(
                low, odd, pltpu.roll(later, zdev, 1)
            )
            tables[2 * side + 1, pl.ds(half + at, BLOCK), :] = jnp.where(low, turned_odd, later)
        return carry

    lax.fori_loop(0, blocks, build, 0)

    own_idx.wait()
    other_idx.wait()
    send_wgt.wait_recv()

    def gather(quarter, first):
        base = quarter * npq + first

        def rows(group, carry):
            at = pl.multiple_of(group * GROUP, GROUP)
            for r in range(GROUP):
                for q in range(4):
                    index = idx_smem[q * pairs * npq + base + at + r]
                    rows_buf[q, pl.ds(at + r, 1), :] = tables[q, pl.ds(index, 1), :]
            return carry

        lax.fori_loop(0, PIX // GROUP, rows, 0)
        total = None
        for q in range(4):
            turned = rows_buf[q].T
            weights = wgt_mine if q < 2 else wgt_recv
            spot = pl.ds(pl.multiple_of(base, PIX), PIX)
            near = weights[pl.ds(2 * (q % 2), 1), spot]
            far = weights[pl.ds(2 * (q % 2) + 1, 1), spot]
            term = near * turned[:zdev] + far * turned[zdev:]
            total = term if total is None else total + term
        return total

    def part_copy(step, piece):
        return pltpu.make_async_remote_copy(
            stage.at[step - 1, piece],
            arrived.at[step - 1, piece],
            part_send.at[step - 1, piece],
            part_recv.at[step - 1, piece],
            device_id={"angle": 2 * pair_peer(step) + parity},
            device_id_type=MESH,
        )

    def z_copy(step, piece):
        return pltpu.make_async_remote_copy(
            zstage.at[piece, band_peer(step)],
            out_ref.at[here, :, pl.ds(pl.multiple_of(piece * chunk, chunk), chunk)],
            z_send.at[step - 1, piece],
            z_recv.at[step - 1, piece],
            device_id={"rows": band_peer(step)},
            device_id_type=MESH,
        )

    for step in range(1, pairs):

        def others(piece, carry):
            def one(part, carry):
                at = pl.multiple_of(part * PIX, PIX)
                stage[step - 1, piece, :, pl.ds(at, PIX)] = gather(
                    pair_peer(step), piece * chunk + at
                )
                return carry

            lax.fori_loop(0, chunk // PIX, one, 0)
            part_copy(step, piece).start()
            return carry

        lax.fori_loop(0, chunks, others, 0)

    def own(piece, carry):
        for step in range(1, pairs):
            part_copy(step, piece).wait_recv()

        def one(part, carry):
            at = pl.multiple_of(part * PIX, PIX)
            total = gather(my_pair, piece * chunk + at)
            for step in range(1, pairs):
                total = total + arrived[step - 1, piece, :, pl.ds(at, PIX)]
            for b in range(bands):
                zstage[piece, b, :, pl.ds(at, PIX)] = total[b * capacity : (b + 1) * capacity]
            return carry

        lax.fori_loop(0, chunk // PIX, one, 0)
        for step in range(1, bands):
            z_copy(step, piece).start()
        spot = pl.ds(pl.multiple_of(piece * chunk, chunk), chunk)
        out_ref[here, :, spot] = zstage[piece, here]
        return carry

    lax.fori_loop(0, chunks, own, 0)

    send_idx.wait_send()
    send_wgt.wait_send()

    def drain(piece, carry):
        for step in range(1, pairs):
            part_copy(step, piece).wait_send()
        for step in range(1, bands):
            z_copy(step, piece).wait()
        return carry

    lax.fori_loop(0, chunks, drain, 0)


def local(projections, rowmap, offsets, fractions, distance_weight):
    bands = lax.axis_size("rows")
    angles = lax.axis_size("angle")
    here = lax.axis_index("rows")
    parity = lax.rem(lax.axis_index("angle"), 2)
    _, band, width = projections.shape
    zdev = rowmap.shape[1] // bands
    capacity = zdev // bands
    pixels = offsets.shape[1]
    npq = pixels // angles
    pairs = angles // 2
    chunk = min(512, npq)
    chunks = npq // chunk
    half = width // 2

    chosen = lax.dynamic_slice_in_dim(
        rowmap.reshape(2, bands, zdev), here * capacity, capacity, 2
    ).reshape(2 * zdev, 1) - here * band

    index = (offsets % 2) * half + offsets // 2
    index = index.reshape(2, pairs, 2, npq)
    weights = jnp.stack(
        [distance_weight * (1.0 - fractions), distance_weight * fractions], axis=1
    ).reshape(4, pairs, 2, npq)

    def of_parity(array, which):
        return lax.dynamic_index_in_dim(array, which, 2, keepdims=False)

    idx_mine = of_parity(index, parity).reshape(-1)
    idx_theirs = of_parity(index, 1 - parity).reshape(-1)
    wgt_mine = of_parity(weights, parity).reshape(4, pairs * npq)
    wgt_theirs = of_parity(weights, 1 - parity).reshape(4, pairs * npq)
    ramp = jnp.asarray(odd_lag_tables(width))

    dims = (angles, bands, band, width, zdev, npq, chunk)
    vmem = pl.BlockSpec(memory_space=pltpu.VMEM)
    rows2 = 2 * zdev
    peers = max(pairs - 1, 1)
    out = pl.pallas_call(
        functools.partial(kernel, dims),
        out_shape=jax.ShapeDtypeStruct((bands, capacity, npq), jnp.float32),
        in_specs=[vmem] * 7,
        out_specs=vmem,
        scratch_shapes=[
            pltpu.VMEM((2, half, 2 * rows2), jnp.bfloat16),
            pltpu.VMEM((half + 8, 2 * rows2), jnp.float32),
            pltpu.VMEM((half, 2 * rows2), jnp.float32),
            pltpu.VMEM((4, width, rows2), jnp.float32),
            pltpu.SMEM((4 * pairs * npq,), jnp.int32),
            pltpu.VMEM((2 * pairs * npq,), jnp.int32),
            pltpu.VMEM((4, pairs * npq), jnp.float32),
            pltpu.VMEM((4, PIX, rows2), jnp.float32),
            pltpu.VMEM((peers, chunks, zdev, chunk), jnp.float32),
            pltpu.VMEM((peers, chunks, zdev, chunk), jnp.float32),
            pltpu.VMEM((chunks, bands, capacity, chunk), jnp.float32),
            pltpu.SemaphoreType.DMA,
            pltpu.SemaphoreType.DMA,
            pltpu.SemaphoreType.DMA((4,)),
            pltpu.SemaphoreType.DMA((peers, chunks)),
            pltpu.SemaphoreType.DMA((peers, chunks)),
            pltpu.SemaphoreType.DMA((max(bands - 1, 1), chunks)),
            pltpu.SemaphoreType.DMA((max(bands - 1, 1), chunks)),
            pltpu.SemaphoreType.DMA((2,)),
        ],
        compiler_params=pltpu.CompilerParams(
            collective_id=0, has_side_effects=True, vmem_limit_bytes=56 * 1024 * 1024
        ),
    )(projections, chosen, ramp, idx_mine, idx_theirs, wgt_mine, wgt_theirs)
    return out.reshape(zdev, npq)


def solution(mesh):
    in_specs = (
        P(("groups", "angle"), "rows", None),
        P(("groups", "angle"), None),
        P(("groups", "angle"), None),
        P(("groups", "angle"), None),
        P(("groups", "angle"), None),
    )
    out_specs = P(("groups", "rows"), "angle")
    return jax.shard_map(local, mesh=mesh, in_specs=in_specs, out_specs=out_specs, check_vma=False)
```

time: 362 us -> 53.5 us (0.15); the launches traced: 355 us -> 53.2 us
  local copies, waits for them, and re-layouts: 170 us -> 6.13 us
  waiting for transfers between devices: 69.2 us -> 0 us
  matrix products: 65.7 us -> 0 us
  Pallas kernels: 0 us -> 44.9 us
  other arithmetic: 29.4 us -> 2.14 us
  between operations: 14 us -> 0.05 us
  starting transfers between devices: 6.32 us -> 0 us
    gather x3 -> x0, local copies, waits for them, and re-layouts: 164 us -> none  [the longest x1 159 us: view_terms(): both = jnp.take(paired, offset, axis=0).astype(jnp.float32)]
    dot_general x8 -> x0, matrix products: 65.7 us -> none  [ramp_filter(): pieces.append(jnp.dot(flat, table, preferred_element_type=jnp.float32))]
    pallas_call x0 -> x1, Pallas kernels: none -> 44.9 us  [local(): pl.pallas_call(functools.partial(kernel, dims), out_shape=jax.ShapeDtypeS...]
    reduce_scatter x1 -> x0, waiting for transfers between devices: 43.8 us -> none  [local(): lax.psum_scatter(partial_sum, 'angle', scatter_dimension=1, tiled=True)]
    all_to_all x1 -> x0, waiting for transfers between devices: 25.4 us -> none  [local(): lax.all_to_all(picked, 'rows', split_axis=1, concat_axis=1, tiled=True)]
    reduce_sum x1 -> x0, other arithmetic: 14.2 us -> none  [backproject(): return jnp.sum(terms, axis=0).T]
    convert_element_type x2 -> x0, other arithmetic: 8.68 us -> none  [the longest x1 6.06 us: view_terms(): both = jnp.take(paired, offset, axis=0).astype(jnp.float32)]
    all_to_all x1 -> x0, starting transfers between devices: 6.32 us -> none  [local(): lax.all_to_all(picked, 'rows', split_axis=1, concat_axis=1, tiled=True)]
  transfers between devices with their start and end apart: 2 -> 0, of which waited for: 2 -> 0; matrix products, arithmetic and copies ran while one was open for 0% -> 0% of each run, Pallas kernels for 0% -> 0%
where the time goes in v1:
time: 53.5 us; the launch traced here: 53.2 us
  Pallas kernels  44.9 us (84%)
  local copies, waits for them, and re-layouts  6.13 us (11%)
  other arithmetic  2.14 us (4%)
    pallas_call x1, Pallas kernels, local(): pl.pallas_call(functools.partial(kernel, dims), out_shape=jax.ShapeDtypeS...  44.9 us
    unnamed x3, local copies, waits for them, and re-layouts  3.2 us
    dynamic_slice x2, local copies, waits for them, and re-layouts, of_parity(): return lax.dynamic_index_in_dim(array, which, 2, keepdims=False)  1.1 us
    add x1, other arithmetic, local(): index = offsets % 2 * half + offsets // 2  1.08 us

profile of v1, /device:TPU:0, one launch (start us, length us, event | category | flops | bytes accessed | tf_op | source)
XLA Modules:
  0.0 53.2 jit_solution(3055088462344393075)
XLA Ops:
  0.0 0.8 %reshape.43 = s32[2,4,64]{2,1,0:T(4,128)S(1)} reshape(s32[2,256]{1,0:T(2,128)} %param.7) | data formatting | bytes 4096 | tf_op jit(solution)/shard_map/reshape | solution.py:314
  0.8 0.1 dynamic-slice_subtract_fusion
  0.8 0.7 %sub.31.chosen_ref = s32[128,1]{1,0:T(8,128)} reshape(s32[2,4,16]{2,1,0:T(4,128)S(1)} %dynamic-slice_subtract_fusion) | data formatting | bytes 1024 | tf_op jit(solution)/shard_map/sub | solution.py:313
  1.6 1.1 %fusion.1 = s32[2,8192]{1,0:T(2,128)S(1)} fusion(s32[2,8192]{1,0:T(2,128)} %param.8), kind=kLoop, calls=%fused_computation.7 | loop fusion | flops 344064 | bytes 131072 | tf_op jit(solution)/shard_map/add | solution.py:317
  2.6 0.1 reshape.44
  2.7 0.7 %constant_dynamic-slice_fusion = (s32[2,2,1,2048]{3,2,1,0:T(1,128)}, s32[2,2,1,2048]{3,2,1,0:T(1,128)}) fusion(s32[2,2,2,2048]{3,2,1,0:T(2,128)S(1)} %reshape.44, s32[]{:T(128)S(6)} %select_n.29, s32[]{:T(128)S(6)} %select_n.28), kind=kLoop, calls=%fused_computation.13 | loop fusion | bytes 131080 | tf_op jit(solution)/shard_map/jit(dynamic_index_in_dim)/dynamic_slice | solution.py:324
  3.4 0.9 %multiply_bitcast_fusion.1 = (f32[2,1,8192]{2,0,1:T(2,128)S(1)}, f32[2,1,8192]{2,0,1:T(2,128)S(1)}) fusion(f32[2,8192]{1,0:T(2,128)} %param.10, f32[2,8192]{1,0:T(2,128)} %param.9), kind=kLoop, calls=%fused_computation.11 | loop fusion | flops 49152 | bytes 262144 | tf_op jit(solution)/shard_map/stack | solution.py:319
  4.4 0.1 pad_maximum_fusion
  4.4 0.1 copy.8
  4.5 0.2 reshape.47
  4.7 0.4 dynamic-slice_reduce_fusion
  5.1 0.7 %copy.11 = f32[1,4,2,2048]{3,1,2,0:T(4,128)} copy(f32[1,4,2,2048]{3,2,1,0:T(2,128)S(1)} %bitcast.15) | data formatting | bytes 131072
  5.8 0.7 %copy.10 = f32[1,4,2,2048]{3,1,2,0:T(4,128)} copy(f32[1,4,2,2048]{3,2,1,0:T(2,128)S(1)} %bitcast.14) | data formatting | bytes 131072
  6.4 44.9 %shard_map.64 = f32[4,16,2048]{2,1,0:T(8,128)} custom-call(f32[2,128,4096]{2,1,0:T(8,128)} %x_ref.1, s32[128,1]{1,0:T(8,128)} %sub.31.chosen_ref, bf16[2,256,3840]{2,1,0:T(8,128)(2,1)} %constant.63.clone.ramp_ref, s32[8192]{0:T(1024)} %bitcast.17, s32[8192]{0:T(1024)} %bitcast.16, f32[4,4096]{1,0:T(4,128)} %bitcast.13, f32[4,4096]{1,0:T(4,128)} %bitcast.12), custom_call_target="tpu_custom_call" | custom-call | tf_op jit(solution)/shard_map/pallas_call | solution.py:336
  51.3 1.9 %copy.13 = f32[64,2048]{1,0:T(8,128)} copy(f32[64,2048]{1,0:T(8,128)} %bitcast.11) | data formatting | bytes 1048576

commit v2 on v1

v2 whole, which is shorter than its diff:
```python
import functools
import math

import jax
import jax.numpy as jnp
import ml_dtypes
import numpy as np
from jax import lax
from jax.experimental import pallas as pl
from jax.experimental.pallas import tpu as pltpu
from jax.sharding import PartitionSpec as P

BLOCK = 256
PIX = 128
GROUP = 32
MESH = pl.DeviceIdType.MESH


def ramp_values(lag):
    magnitude = np.abs(lag)
    spread = np.maximum(magnitude, 1).astype(np.float32)
    odd_term = np.float32(-1.0) / (np.float32(math.pi**2) * spread * spread)
    value = np.where(magnitude % 2 == 1, odd_term, np.float32(0.0))
    return value.astype(ml_dtypes.bfloat16)


def odd_lag_tables(width):
    half = width // 2
    blocks = half // BLOCK
    row = np.arange(BLOCK)[:, None]
    column = np.arange((2 * blocks - 1) * BLOCK)[None, :] - (blocks - 1) * BLOCK
    difference = row - column
    return np.stack([ramp_values(2 * difference - 1), ramp_values(2 * difference + 1)])


def kernel(
    dims,
    x_hbm,
    rowmap_ref,
    offsets_hbm,
    fractions_hbm,
    weight_hbm,
    ramp_hbm,
    out_ref,
    x_buf,
    ramp_buf,
    off_own,
    off_other,
    off_recv,
    frac_own,
    frac_other,
    dist_own,
    dist_other,
    onehot,
    select,
    xt,
    te,
    to,
    tables,
    rows_buf,
    mine,
    stage,
    arrived,
    zstage,
    x_sems,
    in_sems,
    small_sems,
    xt_send,
    xt_recv,
    part_send,
    part_recv,
    z_send,
    z_recv,
):
    angles, bands, band, width, zdev, npq, chunk = dims
    pairs = angles // 2
    capacity = zdev // bands
    chunks = npq // chunk
    half = width // 2
    height = band * bands
    rows2 = 2 * zdev
    slices = 4
    columns = width // slices
    me = lax.axis_index("angle")
    here = lax.axis_index("rows")
    my_pair = me // 2
    parity = me - 2 * my_pair
    partner = {"angle": 2 * my_pair + 1 - parity}

    def pair_peer(step):
        return lax.rem(my_pair + step, pairs)

    def band_peer(step):
        return lax.rem(here + step, bands)

    barrier = pltpu.get_barrier_semaphore()
    pl.semaphore_signal(barrier, inc=1, device_id=partner, device_id_type=MESH)
    for step in range(1, pairs):
        pl.semaphore_signal(
            barrier,
            inc=1,
            device_id={"angle": 2 * pair_peer(step) + parity},
            device_id_type=MESH,
        )
    for step in range(1, bands):
        pl.semaphore_signal(
            barrier, inc=1, device_id={"rows": band_peer(step)}, device_id_type=MESH
        )

    def x_copy(part):
        spot = pl.ds(part * columns, columns)
        return pltpu.make_async_copy(
            x_hbm.at[:, :, spot], x_buf.at[:, :, spot], x_sems.at[part]
        )

    for part in range(slices):
        x_copy(part).start()
    inputs = [
        pltpu.make_async_copy(ramp_hbm, ramp_buf, in_sems.at[0]),
        pltpu.make_async_copy(offsets_hbm, off_own, in_sems.at[1]),
        pltpu.make_async_copy(fractions_hbm, frac_own, in_sems.at[2]),
        pltpu.make_async_copy(weight_hbm, dist_own, in_sems.at[3]),
    ]
    for copy in inputs:
        copy.start()

    row_of = lax.broadcasted_iota(jnp.int32, (band, rowmap_ref.shape[1]), 0) + here * band
    for p in range(2):
        hit = (rowmap_ref[p : p + 1, :] == row_of).astype(jnp.float32)
        onehot[p] = hit.T
        for slab in range(bands):
            for m in range(capacity):
                spot = slab * capacity + m
                select[p, spot : spot + 1, :] = onehot[
                    p, pl.ds(slab * zdev + here * capacity + m, 1), :
                ]
    chosen = [select[p].astype(jnp.bfloat16) for p in range(2)]

    pl.semaphore_wait(barrier, pairs + bands - 1)

    def to_partner(src, dst, at):
        return pltpu.make_async_remote_copy(
            src,
            dst,
            small_sems.at[0, at],
            small_sems.at[1, at],
            device_id=partner,
            device_id_type=MESH,
        )

    small = [
        to_partner(offsets_hbm, off_recv, 0),
        to_partner(fractions_hbm, frac_other, 1),
        to_partner(weight_hbm, dist_other, 2),
    ]
    for copy in small:
        copy.start()

    target = lax.broadcasted_iota(jnp.int32, (BLOCK, BLOCK), 0)
    source = lax.broadcasted_iota(jnp.int32, (BLOCK, BLOCK), 1)
    wanted = jnp.where(target < BLOCK // 2, 2 * target, 2 * target - BLOCK + 1)
    unshuffle = (wanted == source).astype(jnp.bfloat16)
    row_value = (here * band + lax.broadcasted_iota(jnp.int32, (band, 1), 0)).astype(jnp.float32)
    vertical = row_value - (height - 1) / 2.0
    vertical_square = vertical * vertical
    distance = 2.0 * width

    def xt_copy(part):
        spot = pl.ds(part * (columns // 2), columns // 2)
        return pltpu.make_async_remote_copy(
            xt.at[:, spot, pl.ds(0, rows2)],
            xt.at[:, spot, pl.ds(rows2, rows2)],
            xt_send.at[part],
            xt_recv.at[part],
            device_id=partner,
            device_id_type=MESH,
        )

    for part in range(slices):
        x_copy(part).wait()
        for block in range(part * columns // BLOCK, (part + 1) * columns // BLOCK):
            first = block * BLOCK
            column = lax.broadcasted_iota(jnp.int32, (1, BLOCK), 1).astype(jnp.float32) + (
                first - (width - 1) / 2.0
            )
            cosine = distance / jnp.sqrt(distance * distance + column * column + vertical_square)
            picked = []
            for p in range(2):
                weighted = (x_buf[p, :, first : first + BLOCK] * cosine).astype(jnp.bfloat16)
                picked.append(jnp.dot(chosen[p], weighted, preferred_element_type=jnp.float32))
            picked = jnp.concatenate(picked, axis=0).astype(jnp.bfloat16)
            turned = lax.dot_general(
                unshuffle, picked, (((1,), (1,)), ((), ())), preferred_element_type=jnp.float32
            ).astype(jnp.bfloat16)
            at = block * (BLOCK // 2)
            xt[0, at : at + BLOCK // 2, 0:rows2] = turned[: BLOCK // 2]
            xt[1, at : at + BLOCK // 2, 0:rows2] = turned[BLOCK // 2 :]
        xt_copy(part).start()

    small[0].wait_recv()
    last_input = pltpu.make_async_copy(off_recv, off_other, in_sems.at[4])
    last_input.start()
    inputs[0].wait()
    for part in range(slices):
        xt_copy(part).wait_recv()

    low = lax.broadcasted_iota(jnp.int32, (BLOCK, rows2), 1) < zdev
    te[half : half + 8, :] = jnp.zeros((8, 2 * rows2), jnp.float32)
    blocks = half // BLOCK
    for block in reversed(range(blocks)):
        start = (blocks - 1 - block) * BLOCK
        at = block * BLOCK
        for side, out in ((0, te), (1, to)):
            total = jnp.dot(
                ramp_buf[side, :, start : start + half],
                xt[1 - side],
                preferred_element_type=jnp.float32,
            )
            total = total + 0.25 * xt[side, at : at + BLOCK, :].astype(jnp.float32)
            out[at : at + BLOCK, :] = total.astype(jnp.bfloat16).astype(jnp.float32)
        for side in range(2):
            lanes = slice(side * rows2, (side + 1) * rows2)
            even = te[at : at + BLOCK, lanes]
            odd = to[at : at + BLOCK, lanes]
            later = te[at + 1 : at + 1 + BLOCK, lanes]
            turned_odd = pltpu.roll(odd, zdev, 1)
            evens = pl.ds(2 * at, BLOCK, stride=2)
            odds = pl.ds(2 * at + 1, BLOCK, stride=2)
            tables[2 * side, evens, :] = jnp.where(low, even, turned_odd)
            tables[2 * side + 1, evens, :] = jnp.where(low, pltpu.roll(even, zdev, 1), odd)
            tables[2 * side, odds, :] = jnp.where(low, odd, pltpu.roll(later, zdev, 1))
            tables[2 * side + 1, odds, :] = jnp.where(low, turned_odd, later)

    for copy in inputs[1:] + [last_input]:
        copy.wait()
    for copy in small[1:]:
        copy.wait_recv()

    def gather(pair, first):
        base = (2 * pair + parity) * npq + first

        def rows(group, carry):
            at = pl.multiple_of(group * GROUP, GROUP)
            for r in range(GROUP):
                for q in range(4):
                    offsets = off_own if q < 2 else off_other
                    index = offsets[q % 2, base + at + r]
                    rows_buf[q, pl.ds(at + r, 1), :] = tables[q, pl.ds(index, 1), :]
            return carry

        lax.fori_loop(0, PIX // GROUP, rows, 0)
        total = None
        spot = pl.ds(pl.multiple_of(base, PIX), PIX)
        for q in range(4):
            turned = rows_buf[q].T
            fractions = (frac_own if q < 2 else frac_other)[pl.ds(q % 2, 1), spot]
            weight = (dist_own if q < 2 else dist_other)[pl.ds(q % 2, 1), spot]
            near = weight * (1.0 - fractions)
            far = weight * fractions
            term = near * turned[:zdev] + far * turned[zdev:]
            total = term if total is None else total + term
        return total

    def part_copy(step, piece):
        return pltpu.make_async_remote_copy(
            stage.at[step - 1, piece],
            arrived.at[step - 1, piece],
            part_send.at[step - 1, piece],
            part_recv.at[step - 1, piece],
            device_id={"angle": 2 * pair_peer(step) + parity},
            device_id_type=MESH,
        )

    def z_copy(step, piece):
        return pltpu.make_async_remote_copy(
            zstage.at[piece, band_peer(step)],
            out_ref.at[here, :, pl.ds(pl.multiple_of(piece * chunk, chunk), chunk)],
            z_send.at[step - 1, piece],
            z_recv.at[step - 1, piece],
            device_id={"rows": band_peer(step)},
            device_id_type=MESH,
        )

    for step in range(1, pairs):

        def others(piece, carry):
            for part in range(chunk // PIX):
                at = part * PIX
                stage[step - 1, piece, :, at : at + PIX] = gather(
                    pair_peer(step), piece * chunk + at
                )
            part_copy(step, piece).start()
            return carry

        lax.fori_loop(0, chunks, others, 0)

    def own(piece, carry):
        for part in range(chunk // PIX):
            at = part * PIX
            mine[piece, :, at : at + PIX] = gather(my_pair, piece * chunk + at)
        return carry

    lax.fori_loop(0, chunks, own, 0)

    def combine(piece, carry):
        total = mine[piece]
        for step in range(1, pairs):
            part_copy(step, piece).wait_recv()
            total = total + arrived[step - 1, piece]
        for b in range(bands):
            zstage[piece, b] = total[b * capacity : (b + 1) * capacity]
        for step in range(1, bands):
            z_copy(step, piece).start()
        spot = pl.ds(pl.multiple_of(piece * chunk, chunk), chunk)
        out_ref[here, :, spot] = zstage[piece, here]
        return carry

    lax.fori_loop(0, chunks, combine, 0)

    for copy in small:
        copy.wait_send()
    for part in range(slices):
        xt_copy(part).wait_send()

    def drain(piece, carry):
        for step in range(1, pairs):
            part_copy(step, piece).wait_send()
        for step in range(1, bands):
            z_copy(step, piece).wait()
        return carry

    lax.fori_loop(0, chunks, drain, 0)


def local(projections, rowmap, offsets, fractions, distance_weight):
    bands = lax.axis_size("rows")
    angles = lax.axis_size("angle")
    _, band, width = projections.shape
    planes = rowmap.shape[1]
    zdev = planes // bands
    capacity = zdev // bands
    pixels = offsets.shape[1]
    npq = pixels // angles
    pairs = angles // 2
    chunk = min(256, npq)
    chunks = npq // chunk
    half = width // 2
    ramp = jnp.asarray(odd_lag_tables(width))

    dims = (angles, bands, band, width, zdev, npq, chunk)
    vmem = pl.BlockSpec(memory_space=pltpu.VMEM)
    hbm = pl.BlockSpec(memory_space=pl.ANY)
    rows2 = 2 * zdev
    peers = max(pairs - 1, 1)
    small = pltpu.VMEM((2, pixels), jnp.float32)
    out = pl.pallas_call(
        functools.partial(kernel, dims),
        out_shape=jax.ShapeDtypeStruct((bands, capacity, npq), jnp.float32),
        in_specs=[hbm, vmem, hbm, hbm, hbm, hbm],
        out_specs=vmem,
        scratch_shapes=[
            pltpu.VMEM((2, band, width), jnp.float32),
            pltpu.VMEM(ramp.shape, jnp.bfloat16),
            pltpu.SMEM((2, pixels), jnp.int32),
            pltpu.SMEM((2, pixels), jnp.int32),
            pltpu.VMEM((2, pixels), jnp.int32),
            small,
            small,
            small,
            small,
            pltpu.VMEM((2, planes, band), jnp.float32),
            pltpu.VMEM((2, zdev, band), jnp.float32),
            pltpu.VMEM((2, half, 2 * rows2), jnp.bfloat16),
            pltpu.VMEM((half + 8, 2 * rows2), jnp.float32),
            pltpu.VMEM((half, 2 * rows2), jnp.float32),
            pltpu.VMEM((4, width, rows2), jnp.float32),
            pltpu.VMEM((4, PIX, rows2), jnp.float32),
            pltpu.VMEM((chunks, zdev, chunk), jnp.float32),
            pltpu.VMEM((peers, chunks, zdev, chunk), jnp.float32),
            pltpu.VMEM((peers, chunks, zdev, chunk), jnp.float32),
            pltpu.VMEM((chunks, bands, capacity, chunk), jnp.float32),
            pltpu.SemaphoreType.DMA((4,)),
            pltpu.SemaphoreType.DMA((5,)),
            pltpu.SemaphoreType.DMA((2, 3)),
            pltpu.SemaphoreType.DMA((4,)),
            pltpu.SemaphoreType.DMA((4,)),
            pltpu.SemaphoreType.DMA((peers, chunks)),
            pltpu.SemaphoreType.DMA((peers, chunks)),
            pltpu.SemaphoreType.DMA((max(bands - 1, 1), chunks)),
            pltpu.SemaphoreType.DMA((max(bands - 1, 1), chunks)),
        ],
        compiler_params=pltpu.CompilerParams(
            collective_id=0, has_side_effects=True, vmem_limit_bytes=56 * 1024 * 1024
        ),
    )(projections, rowmap, offsets, fractions, distance_weight, ramp)
    return out.reshape(zdev, npq)


def solution(mesh):
    in_specs = (
        P(("groups", "angle"), "rows", None),
        P(("groups", "angle"), None),
        P(("groups", "angle"), None),
        P(("groups", "angle"), None),
        P(("groups", "angle"), None),
    )
    out_specs = P(("groups", "rows"), "angle")
    return jax.shard_map(local, mesh=mesh, in_specs=in_specs, out_specs=out_specs, check_vma=False)
```

time: 53.5 us -> 52.4 us (0.979)
  Pallas kernels: 44.9 us -> 50.4 us
  local copies, waits for them, and re-layouts: 6.13 us -> 1.87 us
  other arithmetic: 2.14 us -> 0 us
    pallas_call x1, Pallas kernels: 44.9 us -> 50.4 us  [local(): pl.pallas_call(functools.partial(kernel, dims), out_shape=jax.ShapeDtypeS...]
    unnamed x3 -> x1, local copies, waits for them, and re-layouts: 3.2 us -> 1.87 us
    dynamic_slice x2 -> x0, local copies, waits for them, and re-layouts: 1.1 us -> none  [of_parity(): return lax.dynamic_index_in_dim(array, which, 2, keepdims=False)]
    add x1 -> x0, other arithmetic: 1.08 us -> none  [local(): index = offsets % 2 * half + offsets // 2]
    reshape x3 -> x0, local copies, waits for them, and re-layouts: 1 us -> none  [the longest x1 0.76 us: local(): rowmap.reshape(2, bands, zdev)]
    another operation x2 -> x0, other arithmetic: 0.99 us -> none  [local(): jnp.stack([distance_weight * (1.0 - fractions), distance_weight * fractio...]
    sub x1 -> x0, local copies, waits for them, and re-layouts: 0.72 us -> none  [local(): lax.dynamic_slice_in_dim(rowmap.reshape(2, bands, zdev), here * capacity,...]
where the time goes in v2:
time: 52.4 us; the launch traced here: 52.2 us
  Pallas kernels  50.4 us (96%)
  local copies, waits for them, and re-layouts  1.87 us (4%)
    pallas_call x1, Pallas kernels, local(): pl.pallas_call(functools.partial(kernel, dims), out_shape=jax.ShapeDtypeS...  50.4 us
    unnamed x1, local copies, waits for them, and re-layouts  1.87 us

profile of v2, /device:TPU:0, one launch (start us, length us, event | category | flops | bytes accessed | tf_op | source)
XLA Modules:
  0.0 52.2 jit_solution(11414013913530378761)
XLA Ops:
  0.0 50.4 %shard_map.64 = f32[4,16,2048]{2,1,0:T(8,128)} custom-call(f32[2,128,4096]{2,1,0:T(8,128)} %x_hbm.1, s32[2,256]{1,0:T(2,128)} %rowmap_ref.1, s32[2,8192]{1,0:T(2,128)} %offsets_hbm.1, f32[2,8192]{1,0:T(2,128)} %fractions_hbm.1, f32[2,8192]{1,0:T(2,128)} %weight_hbm.1, bf16[2,256,3840]{2,1,0:T(8,128)(2,1)} %constant.2.clone.ramp_hbm), custom_call_target="tpu_custom_call" | custom-call | tf_op jit(solution)/shard_map/pallas_call | solution.py:356
  50.4 1.9 %copy.8 = f32[64,2048]{1,0:T(8,128)} copy(f32[64,2048]{1,0:T(8,128)} %bitcast.1) | data formatting | bytes 1048576

commit v3 on v2

--- a/solution.py
+++ b/solution.py
@@ -13,6 +13,7 @@
 BLOCK = 256
 PIX = 128
 GROUP = 32
+LEAD = 2
 MESH = pl.DeviceIdType.MESH
 
 
@@ -46,7 +47,9 @@
     ramp_buf,
     off_own,
     off_other,
+    off_flat,
     off_recv,
+    off_raw,
     frac_own,
     frac_other,
     dist_own,
@@ -117,7 +120,7 @@
         x_copy(part).start()
     inputs = [
         pltpu.make_async_copy(ramp_hbm, ramp_buf, in_sems.at[0]),
-        pltpu.make_async_copy(offsets_hbm, off_own, in_sems.at[1]),
+        pltpu.make_async_copy(offsets_hbm, off_raw, in_sems.at[1]),
         pltpu.make_async_copy(fractions_hbm, frac_own, in_sems.at[2]),
         pltpu.make_async_copy(weight_hbm, dist_own, in_sems.at[3]),
     ]
@@ -136,6 +139,14 @@
                 ]
     chosen = [select[p].astype(jnp.bfloat16) for p in range(2)]
 
+    inputs[1].wait()
+    pixels = off_raw.shape[1]
+    for p in range(2):
+        raw = off_raw[p, :]
+        off_flat[pl.ds(p * pixels, pixels)] = (raw & 1) * half + (raw >> 1)
+    own_offsets = pltpu.make_async_copy(off_flat, off_own, in_sems.at[5])
+    own_offsets.start()
+
     pl.semaphore_wait(barrier, pairs + bands - 1)
 
     def to_partner(src, dst, at):
@@ -149,7 +160,7 @@
         )
 
     small = [
-        to_partner(offsets_hbm, off_recv, 0),
+        to_partner(off_flat, off_recv, 0),
         to_partner(fractions_hbm, frac_other, 1),
         to_partner(weight_hbm, dist_other, 2),
     ]
@@ -224,14 +235,14 @@
             odd = to[at : at + BLOCK, lanes]
             later = te[at + 1 : at + 1 + BLOCK, lanes]
             turned_odd = pltpu.roll(odd, zdev, 1)
-            evens = pl.ds(2 * at, BLOCK, stride=2)
-            odds = pl.ds(2 * at + 1, BLOCK, stride=2)
+            evens = pl.ds(at, BLOCK)
+            odds = pl.ds(half + at, BLOCK)
             tables[2 * side, evens, :] = jnp.where(low, even, turned_odd)
             tables[2 * side + 1, evens, :] = jnp.where(low, pltpu.roll(even, zdev, 1), odd)
             tables[2 * side, odds, :] = jnp.where(low, odd, pltpu.roll(later, zdev, 1))
             tables[2 * side + 1, odds, :] = jnp.where(low, turned_odd, later)
 
-    for copy in inputs[1:] + [last_input]:
+    for copy in inputs[2:] + [own_offsets, last_input]:
         copy.wait()
     for copy in small[1:]:
         copy.wait_recv()
@@ -244,7 +255,7 @@
             for r in range(GROUP):
                 for q in range(4):
                     offsets = off_own if q < 2 else off_other
-                    index = offsets[q % 2, base + at + r]
+                    index = offsets[(q % 2) * pixels + base + at + r]
                     rows_buf[q, pl.ds(at + r, 1), :] = tables[q, pl.ds(index, 1), :]
             return carry
 
@@ -281,29 +292,20 @@
             device_id_type=MESH,
         )
 
-    for step in range(1, pairs):
-
-        def others(piece, carry):
+    def others(piece):
+        for step in range(1, pairs):
             for part in range(chunk // PIX):
                 at = part * PIX
                 stage[step - 1, piece, :, at : at + PIX] = gather(
                     pair_peer(step), piece * chunk + at
                 )
             part_copy(step, piece).start()
-            return carry
-
-        lax.fori_loop(0, chunks, others, 0)
-
-    def own(piece, carry):
+
+    def own(piece):
         for part in range(chunk // PIX):
             at = part * PIX
-            mine[piece, :, at : at + PIX] = gather(my_pair, piece * chunk + at)
-        return carry
-
-    lax.fori_loop(0, chunks, own, 0)
-
-    def combine(piece, carry):
-        total = mine[piece]
+            mine[:, at : at + PIX] = gather(my_pair, piece * chunk + at)
+        total = mine[...]
         for step in range(1, pairs):
             part_copy(step, piece).wait_recv()
             total = total + arrived[step - 1, piece]
@@ -313,9 +315,25 @@
             z_copy(step, piece).start()
         spot = pl.ds(pl.multiple_of(piece * chunk, chunk), chunk)
         out_ref[here, :, spot] = zstage[piece, here]
+
+    lead = min(LEAD, chunks)
+
+    def first_pieces(piece, carry):
+        others(piece)
         return carry
 
-    lax.fori_loop(0, chunks, combine, 0)
+    def both(piece, carry):
+        others(piece + lead)
+        own(piece)
+        return carry
+
+    def last_pieces(piece, carry):
+        own(piece)
+        return carry
+
+    lax.fori_loop(0, lead, first_pieces, 0)
+    lax.fori_loop(0, chunks - lead, both, 0)
+    lax.fori_loop(chunks - lead, chunks, last_pieces, 0)
 
     for copy in small:
         copy.wait_send()
@@ -353,6 +371,7 @@
     rows2 = 2 * zdev
     peers = max(pairs - 1, 1)
     small = pltpu.VMEM((2, pixels), jnp.float32)
+    flat = (2 * pixels,)
     out = pl.pallas_call(
         functools.partial(kernel, dims),
         out_shape=jax.ShapeDtypeStruct((bands, capacity, npq), jnp.float32),
@@ -361,8 +380,10 @@
         scratch_shapes=[
             pltpu.VMEM((2, band, width), jnp.float32),
             pltpu.VMEM(ramp.shape, jnp.bfloat16),
-            pltpu.SMEM((2, pixels), jnp.int32),
-            pltpu.SMEM((2, pixels), jnp.int32),
+            pltpu.SMEM(flat, jnp.int32),
+            pltpu.SMEM(flat, jnp.int32),
+            pltpu.VMEM(flat, jnp.int32),
+            pltpu.VMEM(flat, jnp.int32),
             pltpu.VMEM((2, pixels), jnp.int32),
             small,
             small,
@@ -375,12 +396,12 @@
             pltpu.VMEM((half, 2 * rows2), jnp.float32),
             pltpu.VMEM((4, width, rows2), jnp.float32),
             pltpu.VMEM((4, PIX, rows2), jnp.float32),
-            pltpu.VMEM((chunks, zdev, chunk), jnp.float32),
+            pltpu.VMEM((zdev, chunk), jnp.float32),
             pltpu.VMEM((peers, chunks, zdev, chunk), jnp.float32),
             pltpu.VMEM((peers, chunks, zdev, chunk), jnp.float32),
             pltpu.VMEM((chunks, bands, capacity, chunk), jnp.float32),
             pltpu.SemaphoreType.DMA((4,)),
-            pltpu.SemaphoreType.DMA((5,)),
+            pltpu.SemaphoreType.DMA((6,)),
             pltpu.SemaphoreType.DMA((2, 3)),
             pltpu.SemaphoreType.DMA((4,)),
             pltpu.SemaphoreType.DMA((4,)),

time: 52.4 us -> 40 us (0.76)
  Pallas kernels: 50.4 us -> 38 us
    pallas_call x1, Pallas kernels: 50.4 us -> 38 us  [local(): pl.pallas_call(functools.partial(kernel, dims), out_shape=jax.ShapeDtypeS...]
where the time goes in v3:
time: 40 us; the launch traced here: 39.9 us
  Pallas kernels  38 us (95%)
  local copies, waits for them, and re-layouts  1.87 us (5%)
    pallas_call x1, Pallas kernels, local(): pl.pallas_call(functools.partial(kernel, dims), out_shape=jax.ShapeDtypeS...  38 us
    unnamed x1, local copies, waits for them, and re-layouts  1.87 us

profile of v3, /device:TPU:0, one launch (start us, length us, event | category | flops | bytes accessed | tf_op | source)
XLA Modules:
  0.0 39.9 jit_solution(15754768482981337571)
XLA Ops:
  0.0 38.0 %shard_map.64 = f32[4,16,2048]{2,1,0:T(8,128)} custom-call(f32[2,128,4096]{2,1,0:T(8,128)} %x_hbm.1, s32[2,256]{1,0:T(2,128)} %rowmap_ref.1, s32[2,8192]{1,0:T(2,128)} %offsets_hbm.1, f32[2,8192]{1,0:T(2,128)} %fractions_hbm.1, f32[2,8192]{1,0:T(2,128)} %weight_hbm.1, bf16[2,256,3840]{2,1,0:T(8,128)(2,1)} %constant.2.clone.ramp_hbm), custom_call_target="tpu_custom_call" | custom-call | tf_op jit(solution)/shard_map/pallas_call | solution.py:375
  38.0 1.9 %copy.8 = f32[64,2048]{1,0:T(8,128)} copy(f32[64,2048]{1,0:T(8,128)} %bitcast.1) | data formatting | bytes 1048576

commit v4 on v3

--- a/solution.py
+++ b/solution.py
@@ -14,6 +14,7 @@
 PIX = 128
 GROUP = 32
 LEAD = 2
+LEVELS = 32767.0
 MESH = pl.DeviceIdType.MESH
 
 
@@ -64,7 +65,12 @@
     mine,
     stage,
     arrived,
+    stage_scale,
+    arrived_scale,
     zstage,
+    zscale,
+    zgot,
+    zgot_scale,
     x_sems,
     in_sems,
     small_sems,
@@ -272,22 +278,35 @@
             total = term if total is None else total + term
         return total
 
-    def part_copy(step, piece):
+    def encode(values):
+        most = jnp.maximum(jnp.max(jnp.abs(values), axis=0, keepdims=True), 1e-30)
+        coded = jnp.round(values * (LEVELS / most)).astype(jnp.int32).astype(jnp.int16)
+        return coded, most * (1.0 / LEVELS)
+
+    def decode(coded, scale):
+        return coded.astype(jnp.int32).astype(jnp.float32) * scale
+
+    def part_copy(step, piece, which):
+        src, dst = ((stage, arrived), (stage_scale, arrived_scale))[which]
         return pltpu.make_async_remote_copy(
-            stage.at[step - 1, piece],
-            arrived.at[step - 1, piece],
-            part_send.at[step - 1, piece],
-            part_recv.at[step - 1, piece],
+            src.at[step - 1, piece],
+            dst.at[step - 1, piece],
+            part_send.at[which, step - 1, piece],
+            part_recv.at[which, step - 1, piece],
             device_id={"angle": 2 * pair_peer(step) + parity},
             device_id_type=MESH,
         )
 
-    def z_copy(step, piece):
+    def z_copy(step, piece, which):
+        if which == 0:
+            src, dst = zstage.at[piece, band_peer(step)], zgot.at[step - 1, piece]
+        else:
+            src, dst = zscale.at[piece], zgot_scale.at[step - 1, piece]
         return pltpu.make_async_remote_copy(
-            zstage.at[piece, band_peer(step)],
-            out_ref.at[here, :, pl.ds(pl.multiple_of(piece * chunk, chunk), chunk)],
-            z_send.at[step - 1, piece],
-            z_recv.at[step - 1, piece],
+            src,
+            dst,
+            z_send.at[which, step - 1, piece],
+            z_recv.at[which, step - 1, piece],
             device_id={"rows": band_peer(step)},
             device_id_type=MESH,
         )
@@ -296,10 +315,11 @@
         for step in range(1, pairs):
             for part in range(chunk // PIX):
                 at = part * PIX
-                stage[step - 1, piece, :, at : at + PIX] = gather(
-                    pair_peer(step), piece * chunk + at
-                )
-            part_copy(step, piece).start()
+                coded, scale = encode(gather(pair_peer(step), piece * chunk + at))
+                stage[step - 1, piece, :, at : at + PIX] = coded
+                stage_scale[step - 1, piece, :, at : at + PIX] = scale
+            for which in range(2):
+                part_copy(step, piece, which).start()
 
     def own(piece):
         for part in range(chunk // PIX):
@@ -307,14 +327,24 @@
             mine[:, at : at + PIX] = gather(my_pair, piece * chunk + at)
         total = mine[...]
         for step in range(1, pairs):
-            part_copy(step, piece).wait_recv()
-            total = total + arrived[step - 1, piece]
+            for which in range(2):
+                part_copy(step, piece, which).wait_recv()
+            total = total + decode(arrived[step - 1, piece], arrived_scale[step - 1, piece])
+        mine[...] = total
+        coded, scale = encode(total)
         for b in range(bands):
-            zstage[piece, b] = total[b * capacity : (b + 1) * capacity]
+            zstage[piece, b, 0:capacity] = coded[b * capacity : (b + 1) * capacity]
+        zscale[piece] = scale
         for step in range(1, bands):
-            z_copy(step, piece).start()
+            for which in range(2):
+                z_copy(step, piece, which).start()
         spot = pl.ds(pl.multiple_of(piece * chunk, chunk), chunk)
-        out_ref[here, :, spot] = zstage[piece, here]
+        at = here * capacity
+        if capacity % 8 == 0:
+            out_ref[here, :, spot] = mine[pl.ds(pl.multiple_of(at, 8), capacity), :]
+        else:
+            for m in range(capacity):
+                out_ref[here, m : m + 1, spot] = mine[pl.ds(at + m, 1), :]
 
     lead = min(LEAD, chunks)
 
@@ -341,10 +371,17 @@
         xt_copy(part).wait_send()
 
     def drain(piece, carry):
-        for step in range(1, pairs):
-            part_copy(step, piece).wait_send()
+        for which in range(2):
+            for step in range(1, pairs):
+                part_copy(step, piece, which).wait_send()
+            for step in range(1, bands):
+                z_copy(step, piece, which).wait()
+        spot = pl.ds(pl.multiple_of(piece * chunk, chunk), chunk)
         for step in range(1, bands):
-            z_copy(step, piece).wait()
+            source_band = lax.rem(here + bands - step, bands)
+            out_ref[source_band, :, spot] = decode(
+                zgot[step - 1, piece, 0:capacity], zgot_scale[step - 1, piece]
+            )
         return carry
 
     lax.fori_loop(0, chunks, drain, 0)
@@ -370,6 +407,8 @@
     hbm = pl.BlockSpec(memory_space=pl.ANY)
     rows2 = 2 * zdev
     peers = max(pairs - 1, 1)
+    others = max(bands - 1, 1)
+    padded = -(-capacity // 16) * 16
     small = pltpu.VMEM((2, pixels), jnp.float32)
     flat = (2 * pixels,)
     out = pl.pallas_call(
@@ -397,18 +436,23 @@
             pltpu.VMEM((4, width, rows2), jnp.float32),
             pltpu.VMEM((4, PIX, rows2), jnp.float32),
             pltpu.VMEM((zdev, chunk), jnp.float32),
-            pltpu.VMEM((peers, chunks, zdev, chunk), jnp.float32),
-            pltpu.VMEM((peers, chunks, zdev, chunk), jnp.float32),
-            pltpu.VMEM((chunks, bands, capacity, chunk), jnp.float32),
+            pltpu.VMEM((peers, chunks, zdev, chunk), jnp.int16),
+            pltpu.VMEM((peers, chunks, zdev, chunk), jnp.int16),
+            pltpu.VMEM((peers, chunks, 1, chunk), jnp.float32),
+            pltpu.VMEM((peers, chunks, 1, chunk), jnp.float32),
+            pltpu.VMEM((chunks, bands, padded, chunk), jnp.int16),
+            pltpu.VMEM((chunks, 1, chunk), jnp.float32),
+            pltpu.VMEM((others, chunks, padded, chunk), jnp.int16),
+            pltpu.VMEM((others, chunks, 1, chunk), jnp.float32),
             pltpu.SemaphoreType.DMA((4,)),
             pltpu.SemaphoreType.DMA((6,)),
             pltpu.SemaphoreType.DMA((2, 3)),
             pltpu.SemaphoreType.DMA((4,)),
             pltpu.SemaphoreType.DMA((4,)),
-            pltpu.SemaphoreType.DMA((peers, chunks)),
-            pltpu.SemaphoreType.DMA((peers, chunks)),
-            pltpu.SemaphoreType.DMA((max(bands - 1, 1), chunks)),
-            pltpu.SemaphoreType.DMA((max(bands - 1, 1), chunks)),
+            pltpu.SemaphoreType.DMA((2, peers, chunks)),
+            pltpu.SemaphoreType.DMA((2, peers, chunks)),
+            pltpu.SemaphoreType.DMA((2, others, chunks)),
+            pltpu.SemaphoreType.DMA((2, others, chunks)),
         ],
         compiler_params=pltpu.CompilerParams(
             collective_id=0, has_side_effects=True, vmem_limit_bytes=56 * 1024 * 1024

time: 40 us -> 40 us (level)
  no operation moved by 1% of the time
where the time goes in v4:
time: 40 us; the launch traced here: 39.9 us
  Pallas kernels  38 us (95%)
  local copies, waits for them, and re-layouts  1.87 us (5%)
    pallas_call x1, Pallas kernels, local(): pl.pallas_call(functools.partial(kernel, dims), out_shape=jax.ShapeDtypeS...  38 us
    unnamed x1, local copies, waits for them, and re-layouts  1.87 us

profile of v4, /device:TPU:0, one launch (start us, length us, event | category | flops | bytes accessed | tf_op | source)
XLA Modules:
  0.0 39.9 jit_solution(4830533375339170636)
XLA Ops:
  0.0 38.0 %shard_map.64 = f32[4,16,2048]{2,1,0:T(8,128)} custom-call(f32[2,128,4096]{2,1,0:T(8,128)} %x_hbm.1, s32[2,256]{1,0:T(2,128)} %rowmap_ref.1, s32[2,8192]{1,0:T(2,128)} %offsets_hbm.1, f32[2,8192]{1,0:T(2,128)} %fractions_hbm.1, f32[2,8192]{1,0:T(2,128)} %weight_hbm.1, bf16[2,256,3840]{2,1,0:T(8,128)(2,1)} %constant.2.clone.ramp_hbm), custom_call_target="tpu_custom_call" | custom-call | tf_op jit(solution)/shard_map/pallas_call | solution.py:414
  38.0 1.9 %copy.8 = f32[64,2048]{1,0:T(8,128)} copy(f32[64,2048]{1,0:T(8,128)} %bitcast.1) | data formatting | bytes 1048576

commit v5 on v4

--- a/solution.py
+++ b/solution.py
@@ -13,7 +13,7 @@
 BLOCK = 256
 PIX = 128
 GROUP = 32
-LEAD = 2
+LEAD = 1
 LEVELS = 32767.0
 MESH = pl.DeviceIdType.MESH
 
@@ -397,7 +397,7 @@
     pixels = offsets.shape[1]
     npq = pixels // angles
     pairs = angles // 2
-    chunk = min(256, npq)
+    chunk = min(512, npq)
     chunks = npq // chunk
     half = width // 2
     ramp = jnp.asarray(odd_lag_tables(width))

time: 40 us -> 39 us (0.975)
  Pallas kernels: 38 us -> 37 us
    pallas_call x1, Pallas kernels: 38 us -> 37 us  [local(): pl.pallas_call(functools.partial(kernel, dims), out_shape=jax.ShapeDtypeS...]
where the time goes in v5:
time: 39 us; the launch traced here: 38.9 us
  Pallas kernels  37 us (95%)
  local copies, waits for them, and re-layouts  1.87 us (5%)
    pallas_call x1, Pallas kernels, local(): pl.pallas_call(functools.partial(kernel, dims), out_shape=jax.ShapeDtypeS...  37 us
    unnamed x1, local copies, waits for them, and re-layouts  1.87 us

profile of v5, /device:TPU:0, one launch (start us, length us, event | category | flops | bytes accessed | tf_op | source)
XLA Modules:
  0.0 38.9 jit_solution(11780436564516047914)
XLA Ops:
  0.0 37.0 %shard_map.64 = f32[4,16,2048]{2,1,0:T(8,128)} custom-call(f32[2,128,4096]{2,1,0:T(8,128)} %x_hbm.1, s32[2,256]{1,0:T(2,128)} %rowmap_ref.1, s32[2,8192]{1,0:T(2,128)} %offsets_hbm.1, f32[2,8192]{1,0:T(2,128)} %fractions_hbm.1, f32[2,8192]{1,0:T(2,128)} %weight_hbm.1, bf16[2,256,3840]{2,1,0:T(8,128)(2,1)} %constant.2.clone.ramp_hbm), custom_call_target="tpu_custom_call" | custom-call | tf_op jit(solution)/shard_map/pallas_call | solution.py:414
  37.0 1.9 %copy.8 = f32[64,2048]{1,0:T(8,128)} copy(f32[64,2048]{1,0:T(8,128)} %bitcast.1) | data formatting | bytes 1048576
